TPU v7x, 256 devices: a whole 4x4x8 slice. The times are simulated.
256 devices in a mesh: section: 16 (over x_lo, z), dp: 16 (over x_hi, y, core).
Axes of the slice: x: 4 (x_hi: 2, x_lo: 2; x = x_hi * 2 + x_lo), y: 4, z: 8, core: 2. Of those that a mesh axis runs over, the one named last changes fastest.
Arguments:
- w_value: bfloat16 [16, 2, 2304, 1024], P('section', None, 'dp'), as said below
- w_out_t: bfloat16 [16, 2, 2304, 1024], P('section', None, 'dp'), as said below
- layer_input: bfloat16 [16, 2, 2304, 2048], P('section', None, 'dp'), may hold values from -6 to 6
- grad_out: bfloat16 [16, 2, 2304, 2048], P('section', None, 'dp'), may hold values from -6 to 6
- heads_out: bfloat16 [16, 2048, 2, 1024], P('section', 'dp'), may hold values from -6 to 6
- probs: bfloat16 [16, 2, 8, 2048, 128], P('section', None, None, 'dp'), may hold values from 0 to 1, as said below
Outputs:
- next_down: bfloat16 [16, 2304, 2048], P('section', 'dp')
- next_up: bfloat16 [16, 2304, 2048], P('section', 'dp')
- grad_value: float32 [16, 2304, 1024], P('section', 'dp')
- grad_out_t: float32 [16, 2304, 1024], P('section', 'dp')
Inputs may be any that keep to these rules, and one draw needn't show every extreme that they name: `w_value`: copy 1 of section s equals copy 0 of section 15 - s. `w_out_t`: copy 1 of section s equals copy 0 of section 15 - s. `probs`: within each sequence of 128 tokens a row is zero after the query's own position and sums to one up to bfloat16 rounding.
All inputs are finite; a program needn't handle non-finite values.
Results may differ from a plain program's by a relative error of at most 0.02.
Values may be sent and summed in bfloat16 or wider, within the bound.
A program may use at most 64 MiB of HBM per device.

v0:
```python
import jax
import jax.numpy as jnp
from jax import lax
from jax.sharding import PartitionSpec as P


def from_partner(block, axis, bit):
    count = lax.axis_size(axis)
    route = []
    for low in range(count):
        high = low | 1 << bit
        if high != low and high < count:
            route += [(low, high), (high, low)]
    return lax.ppermute(block, axis, route)


def padded_2(shard, sides, width):
    for axis, dim in sides:
        size, length = (lax.axis_size(axis), shard.shape[dim])
        up = [(i, (i + 1) % size) for i in range(size - 1)]
        down = [(j, i) for i, j in up]
        last = lax.slice_in_dim(shard, length - width, length, axis=dim)
        leading = lax.slice_in_dim(shard, 0, width, axis=dim)
        before = lax.ppermute(last, axis, up)
        after = lax.ppermute(leading, axis, down)
        shard = jnp.concatenate([before, shard, after], axis=dim)
    return shard


def copy_backward(value_weight, out_weight, inputs, grads, heads, weights):
    copies, features, head_width = value_weight.shape
    seq_len = heads.shape[0]
    head_count = weights.shape[1]
    grad_block = grads
    head_sum = lax.psum_scatter(
        jnp.einsum(
            "kft,kfh->tkh", grad_block, out_weight, preferred_element_type=jnp.float32
        ).astype(jnp.bfloat16),
        "dp",
        scatter_dimension=0,
        tiled=True,
    )
    attn_grad = head_sum.reshape(seq_len, copies, head_count, head_width // head_count)
    value_grad = jnp.einsum(
        "khqs,qkhe->skhe", weights, attn_grad, preferred_element_type=jnp.float32
    )
    value_grad = value_grad.astype(jnp.bfloat16).reshape(seq_len, copies, head_width)
    head_piece = lax.all_gather(heads, "dp", axis=0, tiled=True)
    value_piece = lax.all_gather(value_grad, "dp", axis=0, tiled=True)
    grad_block = grads
    out_total = jnp.einsum(
        "kft,tkh->kfh", grad_block, head_piece, preferred_element_type=jnp.float32
    )
    value_total = jnp.einsum(
        "kft,tkh->kfh", inputs, value_piece, preferred_element_type=jnp.float32
    )
    backward = jnp.einsum(
        "kfh,tkh->kft", value_weight, value_piece, preferred_element_type=jnp.float32
    )
    input_grad = backward
    out_total, value_total, input_grad = (out_total, value_total, input_grad)
    passed = (grads.astype(jnp.float32) + input_grad).astype(jnp.bfloat16)
    return (value_total, out_total, passed)


def send_mirror(value_part, out_part, bit_count):
    bit_order = list(range(bit_count))
    for bit_index in bit_order:
        value_part, out_part = (
            from_partner(value_part.astype(jnp.bfloat16), "section", bit_index).astype(
                value_part.dtype
            ),
            from_partner(out_part.astype(jnp.bfloat16), "section", bit_index).astype(
                out_part.dtype
            ),
        )
    return (value_part, out_part)


def on_device(w_value, w_out_t, layer_input, grad_out, heads_out, probs):
    value_weight = w_value[0]
    out_weight = w_out_t[0]
    inputs = layer_input[0]
    grads = grad_out[0]
    heads = heads_out[0]
    weights = probs[0]
    tok_total = grads.shape[2]
    bit_count = lax.axis_size("section").bit_length() - 1
    value_total, out_total, passed = copy_backward(
        value_weight, out_weight, inputs, grads, heads, weights
    )
    mirror_value, mirror_out = send_mirror(value_total[1], out_total[1], bit_count)
    own_value = value_total[0]
    own_out = out_total[0]
    down_grad = passed[0]
    up_grad = passed[1]
    joined = jnp.concatenate([down_grad, up_grad], axis=1)
    padded = padded_2(joined, (("section", 1),), tok_total)
    from_below = padded[:, :tok_total]
    from_above = padded[:, 3 * tok_total :]
    grad_value = own_value + mirror_value
    grad_out_t = own_out + mirror_out
    return (from_above[None], from_below[None], grad_value[None], grad_out_t[None])


def solution(mesh):
    in_specs = (
        P("section", None, "dp", None),
        P("section", None, "dp", None),
        P("section", None, "dp", None),
        P("section", None, "dp", None),
        P("section", "dp", None, None),
        P("section", None, None, "dp", None),
    )
    out_specs = (
        P("section", "dp", None),
        P("section", "dp", None),
        P("section", "dp", None),
        P("section", "dp", None),
    )
    return jax.shard_map(
        on_device, mesh=mesh, in_specs=in_specs, out_specs=out_specs, check_vma=False
    )
```

profile of v0, /device:TPU:64, one launch (start us, length us, event | category | flops | bytes accessed | tf_op | source)
XLA Modules:
  0.0 372.1 jit_solution(3889475505369274250)
XLA Ops:
  7.2 7.2 %convolution_convert_fusion = bf16[2,1024,2048]{2,1,0:T(8,128)(2,1)} fusion(bf16[1,2,144,2048]{3,2,1,0:T(8,128)(2,1)} %param.9, bf16[1,2,144,1024]{3,2,1,0:T(8,128)(2,1)} %param.7), kind=kOutput, calls=%fused_computation.2 | convolution fusion | flops 1212153856 | bytes 10158080 | tf_op jit(solution)/shard_map/kft,kfh->tkh/dot_general | solution.py:36
  14.4 12.4 %copy.16 = bf16[2048,2048]{1,0:T(8,128)(2,1)} copy(bf16[2048,2048]{0,1:T(8,128)(2,1)} %bitcast.68) | data formatting | bytes 16777216
  26.9 1.0 copy-done.5
  27.8 0.9 copy.13
  28.8 110.5 %reduce-scatter.4.cloned.1.call-done = bf16[128,2048]{1,0:T(8,128)(2,1)} async-done(((bf16[2048,2048]{1,0:T(8,128)(2,1)}), bf16[128,2048]{1,0:T(8,128)(2,1)}) %reduce-scatter.4.cloned.1.call-update) | async-done | bytes 524304
  139.3 1.3 copy.17
  140.9 1.0 copy.12
  142.0 77.6 %all-gather.6.cloned.1.call-done = bf16[1,2048,2,1024]{3,1,2,0:T(8,128)(2,1)} async-done(((bf16[1,128,2,1024]{3,1,2,0:T(8,128)(2,1)}), bf16[1,2048,2,1024]{3,1,2,0:T(8,128)(2,1)}) %all-gather.6.cloned.1.call-update) | async-done | bytes 8388624 | tf_op jit(solution)/shard_map/all_gather | solution.py:48
  219.5 4.8 %fusion = f32[2,144,1024]{2,1,0:T(8,128)S(1)} fusion(bf16[1,2048,2,1024]{3,1,2,0:T(8,128)(2,1)} %all-gather.6.cloned.1.call-done, bf16[1,2,144,2048]{3,2,1,0:T(8,128)(2,1)S(1)} %copy-done.2), kind=kOutput, calls=%fused_computation | convolution fusion | flops 1207959552 | bytes 10747904 | tf_op jit(solution)/shard_map/kft,tkh->kfh/dot_general | solution.py:51
  224.3 1.6 collective-permute-start.6
  226.0 7.6 %collective-permute-done.6 = bf16[144,1024]{1,0:T(8,128)(2,1)S(1)} collective-permute-done((bf16[144,1024]{1,0:T(8,128)(2,1)S(1)}, bf16[144,1024]{1,0:T(8,128)(2,1)S(1)}, u32[]{:S(2)}, u32[]{:S(2)}) %collective-permute-start.6) | collective-permute-done | bytes 294944 | tf_op jit(solution)/shard_map/ppermute | solution.py:14
  233.6 0.4 collective-permute-start.7
  234.0 12.2 %collective-permute-done.7 = bf16[144,1024]{1,0:T(8,128)(2,1)} collective-permute-done((bf16[144,1024]{1,0:T(8,128)(2,1)S(1)}, bf16[144,1024]{1,0:T(8,128)(2,1)}, u32[]{:S(2)}, u32[]{:S(2)}) %collective-permute-start.7) | collective-permute-done | bytes 294944 | tf_op jit(solution)/shard_map/ppermute | solution.py:14
  246.2 5.7 %collective-permute-start.8 = (bf16[144,1024]{1,0:T(8,128)(2,1)}, bf16[144,1024]{1,0:T(8,128)(2,1)}, u32[]{:S(2)}, u32[]{:S(2)}) collective-permute-start(bf16[144,1024]{1,0:T(8,128)(2,1)} %collective-permute-done.7), channel_id=1, source_target_pairs={{0,64},{64,0},{16,80},{80,16},{32,96},{96,32},{48,112},{112,48},{1... | collective-permute-start | bytes 884744 | tf_op jit(solution)/shard_map/ppermute | solution.py:14
  251.9 46.9 %all-gather.4.cloned.1.call-done = bf16[2048,2,1024]{2,0,1:T(8,128)(2,1)} async-done(((bf16[128,2,1024]{2,0,1:T(8,128)(2,1)}), bf16[2048,2,1024]{2,0,1:T(8,128)(2,1)}) %all-gather.4.cloned.1.call-update) | async-done | bytes 8388624 | tf_op jit(solution)/shard_map/all_gather | solution.py:49
  298.9 4.9 %convolution_bitcast_fusion.1 = f32[2,144,1024]{2,1,0:T(8,128)S(1)} fusion(bf16[2048,2,1024]{2,0,1:T(8,128)(2,1)} %all-gather.4.cloned.1.call-done, bf16[1,2,144,2048]{3,2,1,0:T(8,128)(2,1)S(1)} %copy-done), kind=kOutput, calls=%fused_computation.6 | convolution fusion | flops 1207959552 | bytes 10747904 | tf_op jit(solution)/shard_map/kft,tkh->kfh/dot_general | solution.py:54
  303.8 1.6 collective-permute-start.2
  305.5 2.9 fusion.3
  308.4 4.7 %collective-permute-done.2 = bf16[144,1024]{1,0:T(8,128)(2,1)S(1)} collective-permute-done((bf16[144,1024]{1,0:T(8,128)(2,1)S(1)}, bf16[144,1024]{1,0:T(8,128)(2,1)S(1)}, u32[]{:S(2)}, u32[]{:S(2)}) %collective-permute-start.2) | collective-permute-done | bytes 294944 | tf_op jit(solution)/shard_map/ppermute | solution.py:14
  313.1 0.4 collective-permute-start.3
  313.6 4.5 %collective-permute-start = (bf16[144,2048]{1,0:T(8,128)(2,1)S(1)}, bf16[144,2048]{1,0:T(8,128)(2,1)S(1)}, u32[]{:S(2)}, u32[]{:S(2)}) collective-permute-start(bf16[144,2048]{1,0:T(8,128)(2,1)S(1)} %get-tuple-element.5), channel_id=1, source_target_pairs={{16,0},{32,16},{48,32},{64,48},{80,64},{96,80},{112,96},{128,112},... | collective-permute-start | bytes 1769480 | tf_op jit(solution)/shard_map/ppermute | solution.py:25
  318.1 1.9 collective-permute-start.1
  320.1 6.8 %collective-permute-done.3 = bf16[144,1024]{1,0:T(8,128)(2,1)S(1)} collective-permute-done((bf16[144,1024]{1,0:T(8,128)(2,1)S(1)}, bf16[144,1024]{1,0:T(8,128)(2,1)S(1)}, u32[]{:S(2)}, u32[]{:S(2)}) %collective-permute-start.3) | collective-permute-done | bytes 294944 | tf_op jit(solution)/shard_map/ppermute | solution.py:14
  326.9 4.8 %collective-permute-start.4 = (bf16[144,1024]{1,0:T(8,128)(2,1)S(1)}, bf16[144,1024]{1,0:T(8,128)(2,1)S(1)}, u32[]{:S(2)}, u32[]{:S(2)}) collective-permute-start(bf16[144,1024]{1,0:T(8,128)(2,1)S(1)} %collective-permute-done.3), channel_id=1, source_target_pairs={{0,64},{64,0},{16,80},{80,16},{32,96},{96,32},{48,112},{112,48},{1... | collective-permute-start | bytes 884744 | tf_op jit(solution)/shard_map/ppermute | solution.py:14
  331.6 0.6 collective-permute-start.9
  332.2 23.1 %collective-permute-done.4 = bf16[144,1024]{1,0:T(8,128)(2,1)S(1)} collective-permute-done((bf16[144,1024]{1,0:T(8,128)(2,1)S(1)}, bf16[144,1024]{1,0:T(8,128)(2,1)S(1)}, u32[]{:S(2)}, u32[]{:S(2)}) %collective-permute-start.4) | collective-permute-done | bytes 294944 | tf_op jit(solution)/shard_map/ppermute | solution.py:14
  355.3 0.6 collective-permute-start.5
  355.9 0.9 fusion.8
  356.8 6.2 %collective-permute-done.5 = bf16[144,1024]{1,0:T(8,128)(2,1)S(1)} collective-permute-done((bf16[144,1024]{1,0:T(8,128)(2,1)S(1)}, bf16[144,1024]{1,0:T(8,128)(2,1)S(1)}, u32[]{:S(2)}, u32[]{:S(2)}) %collective-permute-start.5) | collective-permute-done | bytes 294944 | tf_op jit(solution)/shard_map/ppermute | solution.py:14
  363.0 0.9 fusion.10
  363.9 0.8 copy.20
  364.7 0.8 copy.21
  (25 shorter events, 0.7 us)
Async XLA Ops:
  7.2 291.7 %copy-start = (bf16[1,2,144,2048]{3,2,1,0:T(8,128)(2,1)S(1)}, bf16[1,2,144,2048]{3,2,1,0:T(8,128)(2,1)}, u32[]{:S(2)}) copy-start(bf16[1,2,144,2048]{3,2,1,0:T(8,128)(2,1)} %param.8) | copy-start | bytes 3538948
  7.2 132.1 %reduce-scatter.4.cloned.1.call-start = ((), (), s32[]{:S(2)}) async-start(), calls=%async_computation.3 | async-start | bytes 8912896
  26.8 1.0 copy-start.5
  26.8 113.8 %copy-start.4 = (bf16[1,2,8,128,128]{4,3,2,1,0:T(8,128)(2,1)S(1)}, bf16[1,2,8,128,128]{4,3,2,1,0:T(8,128)(2,1)}, u32[]{:S(2)}) copy-start(bf16[1,2,8,128,128]{4,3,2,1,0:T(8,128)(2,1)} %param.11) | copy-start | bytes 1572868
  26.8 192.7 %all-gather.6.cloned.1.call-start = ((), (), s32[]{:S(2)}) async-start(), calls=%async_computation.2 | async-start | bytes 8912896 | tf_op jit(solution)/shard_map/all_gather | solution.py:48
  28.8 270.1 %all-gather.4.cloned.1.call-start = ((), (), s32[]{:S(2)}) async-start(), calls=%async_computation.1 | async-start | bytes 8912896 | tf_op jit(solution)/shard_map/all_gather | solution.py:49
  140.9 78.6 %copy-start.2 = (bf16[1,2,144,2048]{3,2,1,0:T(8,128)(2,1)S(1)}, bf16[1,2,144,2048]{3,2,1,0:T(8,128)(2,1)}, u32[]{:S(2)}) copy-start(bf16[1,2,144,2048]{3,2,1,0:T(8,128)(2,1)} %param.9) | copy-start | bytes 3538948
  224.3 9.3 %collective-permute-start.6 = (bf16[144,1024]{1,0:T(8,128)(2,1)S(1)}, bf16[144,1024]{1,0:T(8,128)(2,1)S(1)}, u32[]{:S(2)}, u32[]{:S(2)}) collective-permute-start(bf16[144,1024]{1,0:T(8,128)(2,1)S(1)} %fusion.15), channel_id=1, source_target_pairs={{0,16},{16,0},{32,48},{48,32},{64,80},{80,64},{96,112},{112,96},{1... | collective-permute-start | bytes 884744 | tf_op jit(solution)/shard_map/ppermute | solution.py:14
  233.6 12.6 %collective-permute-start.7 = (bf16[144,1024]{1,0:T(8,128)(2,1)S(1)}, bf16[144,1024]{1,0:T(8,128)(2,1)}, u32[]{:S(2)}, u32[]{:S(2)}) collective-permute-start(bf16[144,1024]{1,0:T(8,128)(2,1)S(1)} %collective-permute-done.6), channel_id=1, source_target_pairs={{0,32},{32,0},{16,48},{48,16},{64,96},{96,64},{80,112},{112,80},{1... | collective-permute-start | bytes 884744 | tf_op jit(solution)/shard_map/ppermute | solution.py:14
  246.2 85.4 %collective-permute-start.8 = (bf16[144,1024]{1,0:T(8,128)(2,1)}, bf16[144,1024]{1,0:T(8,128)(2,1)}, u32[]{:S(2)}, u32[]{:S(2)}) collective-permute-start(bf16[144,1024]{1,0:T(8,128)(2,1)} %collective-permute-done.7), channel_id=1, source_target_pairs={{0,64},{64,0},{16,80},{80,16},{32,96},{96,32},{48,112},{112,48},{1... | collective-permute-start | bytes 884744 | tf_op jit(solution)/shard_map/ppermute | solution.py:14
  298.9 6.6 %copy-start.1 = (bf16[2048,2,1024]{2,0,1:T(8,128)(2,1)S(1)}, bf16[2048,2,1024]{2,0,1:T(8,128)(2,1)}, u32[]{:S(2)}) copy-start(bf16[2048,2,1024]{2,0,1:T(8,128)(2,1)} %all-gather.4.cloned.1.call-done) | copy-start | bytes 25165828
  298.9 6.6 %copy-start.3 = (bf16[1,2,144,1024]{3,2,1,0:T(8,128)(2,1)S(1)}, bf16[1,2,144,1024]{3,2,1,0:T(8,128)(2,1)}, u32[]{:S(2)}) copy-start(bf16[1,2,144,1024]{3,2,1,0:T(8,128)(2,1)} %param.6) | copy-start | bytes 1769476
  303.8 9.3 %collective-permute-start.2 = (bf16[144,1024]{1,0:T(8,128)(2,1)S(1)}, bf16[144,1024]{1,0:T(8,128)(2,1)S(1)}, u32[]{:S(2)}, u32[]{:S(2)}) collective-permute-start(bf16[144,1024]{1,0:T(8,128)(2,1)S(1)} %fusion.14), channel_id=1, source_target_pairs={{0,16},{16,0},{32,48},{48,32},{64,80},{80,64},{96,112},{112,96},{1... | collective-permute-start | bytes 884744 | tf_op jit(solution)/shard_map/ppermute | solution.py:14
  313.1 13.8 %collective-permute-start.3 = (bf16[144,1024]{1,0:T(8,128)(2,1)S(1)}, bf16[144,1024]{1,0:T(8,128)(2,1)S(1)}, u32[]{:S(2)}, u32[]{:S(2)}) collective-permute-start(bf16[144,1024]{1,0:T(8,128)(2,1)S(1)} %collective-permute-done.2), channel_id=1, source_target_pairs={{0,32},{32,0},{16,48},{48,16},{64,96},{96,64},{80,112},{112,80},{1... | collective-permute-start | bytes 884744 | tf_op jit(solution)/shard_map/ppermute | solution.py:14
  313.6 43.2 %collective-permute-start = (bf16[144,2048]{1,0:T(8,128)(2,1)S(1)}, bf16[144,2048]{1,0:T(8,128)(2,1)S(1)}, u32[]{:S(2)}, u32[]{:S(2)}) collective-permute-start(bf16[144,2048]{1,0:T(8,128)(2,1)S(1)} %get-tuple-element.5), channel_id=1, source_target_pairs={{16,0},{32,16},{48,32},{64,48},{80,64},{96,80},{112,96},{128,112},... | collective-permute-start | bytes 1769480 | tf_op jit(solution)/shard_map/ppermute | solution.py:25
  318.1 38.7 %collective-permute-start.1 = (bf16[144,2048]{1,0:T(8,128)(2,1)S(1)}, bf16[144,2048]{1,0:T(8,128)(2,1)S(1)}, u32[]{:S(2)}, u32[]{:S(2)}) collective-permute-start(bf16[144,2048]{1,0:T(8,128)(2,1)S(1)} %get-tuple-element.4), channel_id=1, source_target_pairs={{0,16},{16,32},{32,48},{48,64},{64,80},{80,96},{96,112},{112,128},... | collective-permute-start | bytes 1769480 | tf_op jit(solution)/shard_map/ppermute | solution.py:24
  326.9 28.4 %collective-permute-start.4 = (bf16[144,1024]{1,0:T(8,128)(2,1)S(1)}, bf16[144,1024]{1,0:T(8,128)(2,1)S(1)}, u32[]{:S(2)}, u32[]{:S(2)}) collective-permute-start(bf16[144,1024]{1,0:T(8,128)(2,1)S(1)} %collective-permute-done.3), channel_id=1, source_target_pairs={{0,64},{64,0},{16,80},{80,16},{32,96},{96,32},{48,112},{112,48},{1... | collective-permute-start | bytes 884744 | tf_op jit(solution)/shard_map/ppermute | solution.py:14
  331.6 24.3 %collective-permute-start.9 = (bf16[144,1024]{1,0:T(8,128)(2,1)}, bf16[144,1024]{1,0:T(8,128)(2,1)S(1)}, u32[]{:S(2)}, u32[]{:S(2)}) collective-permute-start(bf16[144,1024]{1,0:T(8,128)(2,1)} %collective-permute-done.8), channel_id=1, source_target_pairs={{0,128},{128,0},{16,144},{144,16},{32,160},{160,32},{48,176},{176,... | collective-permute-start | bytes 884744 | tf_op jit(solution)/shard_map/ppermute | solution.py:14
  355.3 7.7 %collective-permute-start.5 = (bf16[144,1024]{1,0:T(8,128)(2,1)S(1)}, bf16[144,1024]{1,0:T(8,128)(2,1)S(1)}, u32[]{:S(2)}, u32[]{:S(2)}) collective-permute-start(bf16[144,1024]{1,0:T(8,128)(2,1)S(1)} %collective-permute-done.4), channel_id=1, source_target_pairs={{0,128},{128,0},{16,144},{144,16},{32,160},{160,32},{48,176},{176,... | collective-permute-start | bytes 884744 | tf_op jit(solution)/shard_map/ppermute | solution.py:14
Sparse Core Ops, SparseCore 0:
  26.9 112.3 reduce-scatter.3
  142.7 76.7 all-gather.5
  222.9 75.8 all-gather.3
where the time goes:
time: 373 us; the launch traced here: 372 us
  waiting for transfers between devices  296 us (79%)
  starting transfers between devices  22.3 us (6%)
  matrix products  20.1 us (5%)
  local copies, waits for them, and re-layouts  18.4 us (5%)
  between operations  13.9 us (4%)
    unnamed x4, waiting for transfers between devices  111 us
    all_gather x1, waiting for transfers between devices, copy_backward(): head_piece = lax.all_gather(heads, 'dp', axis=0, tiled=True)  77.6 us
    ppermute x8, waiting for transfers between devices, from_partner(): return lax.ppermute(block, axis, route)  60.6 us
    all_gather x1, waiting for transfers between devices, copy_backward(): value_piece = lax.all_gather(value_grad, 'dp', axis=0, tiled=True)  46.9 us
    unnamed x17, local copies, waits for them, and re-layouts  17.2 us
    ppermute x8, starting transfers between devices, from_partner(): return lax.ppermute(block, axis, route)  15.7 us
  transfers between devices with their start and end apart: 13, of which 9 were waited for; matrix products, arithmetic and copies ran while one was open for 5% of the time, Pallas kernels for 0%

commit v1 on v0

v1 whole, which is shorter than its diff:
```python
import itertools

import jax
import jax.numpy as jnp
from jax import lax
from jax.experimental import pallas as pl
from jax.experimental.pallas import tpu as pltpu
from jax.sharding import PartitionSpec as P

F = 144
T = 2048
H = 1024
SEQ = 128
HD = 128
HALF = 512
BF = jnp.bfloat16
F32 = jnp.float32
N_SEM = 112
N_LOCAL = 20


def contract(a, b, da, db):
    return lax.dot_general(a, b, (((da,), (db,)), ((), ())), preferred_element_type=F32)


def kernel(
    w_v, w_o, x_in, g_in, hd_in, pr_in,
    nxt, gval, gout,
    gall, goth, wall, hd, sp, own, r1, r2, pb, vall, xb, wvb, vacc, pacc, pbf,
    oacc, obk, orx, ofin, mo_s, mo_r, lo_r, mv_s, mv_r, lv_r, fin_o, fin_v, zero,
    ssem, rsem, lsem,
):
    sec = lax.axis_index("section")
    dp = lax.axis_index("dp")
    xh = dp // 8
    y = (dp // 2) % 4
    k = dp % 2
    o = 1 - k
    xo = 1 - xh
    yp, y2, ym = (y + 1) % 4, (y + 2) % 4, (y + 3) % 4
    around = (y, yp, y2, ym)

    def dev(a, b, c):
        return {"dp": a * 8 + b * 2 + c}

    sib, par, pao = dev(xh, y, o), dev(xo, y, k), dev(xo, y, o)
    up, dn = dev(xh, yp, k), dev(xh, ym, k)
    has_above = sec < 15
    has_below = sec > 0
    is0 = k == 0
    is1 = k == 1
    halo_ok = jnp.logical_or(jnp.logical_and(is0, has_below), jnp.logical_and(is1, has_above))
    halo_sec = jnp.clip(sec - 1 + 2 * k, 0, 15)

    counter = itertools.count()
    locals_ = itertools.count()
    sent = []

    def alloc(n=1):
        first = next(counter)
        for _ in range(n - 1):
            next(counter)
        assert first + n <= N_SEM
        return first

    def remote(src, dst, to, n, m=None):
        return pltpu.make_async_remote_copy(
            src_ref=src, dst_ref=dst, send_sem=ssem.at[n], recv_sem=rsem.at[n if m is None else m],
            device_id=to, device_id_type=pl.DeviceIdType.MESH,
        )

    def push(src, dst, to, n=None):
        copy = remote(src, dst, to, alloc() if n is None else n)
        copy.start()
        sent.append(copy)
        return copy

    def arrive(dst, n):
        remote(dst, dst, sib, n).wait_recv()

    def pull(src, dst):
        copy = pltpu.make_async_copy(src, dst, lsem.at[next(locals_)])
        copy.start()
        return copy

    tcol = xh * 1024
    ocol = xo * 1024

    def cols(base, yy, width=256):
        return pl.ds(pl.multiple_of(base + yy * 256, 256), width)

    own_w = pull(w_o.at[k], wall.at[k])
    own_g = [pull(g_in.at[k, :, cols(tcol, yy)], gall.at[yy, k]) for yy in range(4)]
    own_hd = pull(hd_in.at[k], hd.at[y, k])
    own_rest = [
        pull(pr_in.at[k], pb.at[k]),
        pull(w_v.at[k], wvb.at[k]),
        pull(x_in.at[k], xb.at[k]),
        pull(g_in.at[k, :, cols(ocol, 0, 1024)], goth.at[k]),
    ]

    barrier = pltpu.get_barrier_semaphore()

    def greet(to):
        pl.semaphore_signal(barrier, inc=1, device_id=to, device_id_type=pl.DeviceIdType.MESH)

    for to in (sib, par, pao, up, dn):
        greet(to)
    greet({"section": 15 - sec, "dp": xh * 8 + y * 2 + 1})

    @pl.when(has_above)
    def _():
        greet({"section": jnp.minimum(sec + 1, 15), "dp": xh * 8 + y * 2})

    @pl.when(has_below)
    def _():
        greet({"section": jnp.maximum(sec - 1, 0), "dp": xh * 8 + y * 2 + 1})

    pl.semaphore_wait(barrier, 5 + 2 * k + 2 * halo_ok.astype(jnp.int32))

    h_up, h_dn = alloc(2), alloc(2)
    hd_sib = push(hd_in.at[o], hd.at[y, k], sib)
    push(hd_in.at[k], hd.at[y, k], up, h_up + k)
    push(hd_in.at[k], hd.at[y, k], dn, h_dn + k)
    w_copies = [
        push(w_o.at[o], wall.at[k], sib),
        push(w_o.at[k], wall.at[2 + k], par),
        push(w_o.at[o], wall.at[2 + k], pao),
    ]
    g_copies = {}
    for d in (2, 1, 3, 0):
        yy = around[d]
        g_copies[d] = [
            push(g_in.at[o, :, cols(tcol, yy)], gall.at[yy, k], sib),
            push(g_in.at[k, :, cols(ocol, yy)], gall.at[yy, 2 + k], par),
            push(g_in.at[o, :, cols(ocol, yy)], gall.at[yy, 2 + k], pao),
        ]

    hd_sib.wait_recv()
    push(hd.at[y, o], hd.at[y, o], up, h_up + o)
    push(hd.at[y, o], hd.at[y, o], dn, h_dn + o)
    rest = [
        push(pr_in.at[o], pb.at[k], sib),
        push(w_v.at[o], wvb.at[k], sib),
        push(x_in.at[o], xb.at[k], sib),
        push(g_in.at[o, :, cols(ocol, 0, 1024)], goth.at[k], sib),
    ]

    zero[...] = jnp.zeros_like(zero)
    edge = jnp.where(has_above, 1, 0)
    no_edge = jnp.logical_and(has_above, has_below)
    zero_copy = pltpu.make_async_copy(zero, nxt.at[edge], lsem.at[next(locals_)])

    @pl.when(jnp.logical_not(no_edge))
    def _():
        zero_copy.start()

    arrive(hd.at[ym, 0], h_up)
    hd_f_up = push(hd.at[ym, 0], hd.at[ym, 0], up)
    arrive(hd.at[yp, 1], h_dn + 1)
    hd_f_dn = push(hd.at[yp, 1], hd.at[yp, 1], dn)

    own_w.wait()
    for copy in own_g:
        copy.wait()
    for copy in w_copies:
        copy.wait_recv()

    def partial(d):
        for copy in g_copies[d]:
            copy.wait_recv()
        part = contract(
            gall[around[d]].reshape(4 * F, 256), wall[...].reshape(4 * F, H), 0, 0
        )
        for h in range(2):
            for q in range(2):
                piece = part[q * SEQ : (q + 1) * SEQ, h * HALF : (h + 1) * HALF]
                if d == 0:
                    own[h, q] = piece
                else:
                    sp[d, h, q] = piece.astype(BF)

    def out_term(d, first=False):
        term = contract(
            gall[around[d]].reshape(4 * F, 256), hd[around[d]].reshape(256, H), 1, 0
        )
        if first:
            oacc[...] = term
        else:
            oacc[...] += term

    s1 = {}
    s2 = {}

    def ring_first(h):
        s1[h] = [
            push(sp.at[2, h, 0], r1.at[0, h], up),
            push(sp.at[2, h, 1], r1.at[1, h], dn),
        ]

    def ring_up(h):
        s2[h, 0] = push(sp.at[1, h, 1], r2.at[0, h, 1], up)

    def ring_dn(h):
        s2[h, 1] = push(sp.at[3, h, 0], r2.at[1, h, 0], dn)

    def ring_sum(h):
        s1[h][0].wait_recv()
        sp[1, h, 0] = (sp[1, h, 0].astype(F32) + r1[0, h].astype(F32)).astype(BF)
        s2[h, 2] = push(sp.at[1, h, 0], r2.at[0, h, 0], up)
        s1[h][1].wait_recv()
        sp[3, h, 1] = (sp[3, h, 1].astype(F32) + r1[1, h].astype(F32)).astype(BF)
        s2[h, 3] = push(sp.at[3, h, 1], r2.at[1, h, 1], dn)

    partial(2)
    ring_first(0)
    partial(1)
    ring_up(0)
    own_hd.wait()
    arrive(hd.at[yp, 0], h_dn)
    out_term(1, first=True)
    partial(3)
    ring_dn(0)
    arrive(hd.at[ym, 1], h_up + 1)
    out_term(3)
    ring_sum(0)
    ring_first(1)
    ring_up(1)
    ring_dn(1)
    partial(0)
    out_term(0)
    hd_f_up.wait_recv()
    hd_f_dn.wait_recv()
    out_term(2)
    obk[...] = oacc[2 * F :].astype(BF).reshape(2, F, H)

    for copy in own_rest:
        copy.wait()
    for copy in rest:
        copy.wait_recv()

    v_sent = {}

    def attention(h):
        for i in range(4):
            s2[h, i].wait_recv()
        for q in range(2):
            total = own[h, q] + r2[0, h, q].astype(F32) + r2[1, h, q].astype(F32)
            total = total.astype(BF)
            for e in range(4):
                vall[h, xh, y, q, :, e * HD : (e + 1) * HD] = contract(
                    pb[q, h * 4 + e], total[:, e * HD : (e + 1) * HD], 0, 0
                ).astype(BF)
        mine = vall.at[h, xh, y]
        v_sent[h, "x"] = push(mine, mine, par)
        v_sent[h, 0, "u"] = push(mine, mine, up)
        v_sent[h, 0, "d"] = push(mine, mine, dn)

    def spread_other(h):
        v_sent[h, "x"].wait_recv()
        other = vall.at[h, xo, y]
        v_sent[h, 1, "u"] = push(other, other, up)
        v_sent[h, 1, "d"] = push(other, other, dn)

    def forward(h, side):
        xx = (xh, xo)[side]
        v_sent[h, side, "u"].wait_recv()
        piece = vall.at[h, xx, ym, 0]
        v_sent[h, side, "fu"] = push(piece, piece, up)
        v_sent[h, side, "d"].wait_recv()
        piece = vall.at[h, xx, yp, 1]
        v_sent[h, side, "fd"] = push(piece, piece, dn)

    def far(h, side):
        v_sent[h, side, "fu"].wait_recv()
        v_sent[h, side, "fd"].wait_recv()

    halo_sem = alloc(16)
    halo_send = alloc(16)
    halos = []

    def use(h, side, d, first=False):
        xx, yy = (xh, xo)[side], around[d]
        at = cols(xx * 1024, yy)
        block = vall[h, xx, yy].reshape(256, HALF)
        term = contract(xb[:, :, at].reshape(2 * F, 256), block, 1, 0).reshape(2, F, HALF)
        if first:
            vacc[h] = term
        else:
            vacc[h] += term
        back = contract(
            wvb[:, :, h * HALF : (h + 1) * HALF].reshape(2 * F, HALF), block, 1, 1
        )
        i = side * 4 + d
        if h == 0:
            pacc[i] = back
            return
        g_here = gall[yy, 0:2] if side == 0 else goth[:, :, cols(0, yy)]
        total = g_here.reshape(2 * F, 256).astype(F32) + (pacc[i] + back)
        pbf[i] = total.astype(BF).reshape(2, F, 256)
        copies = [
            remote(
                pbf.at[i, b], nxt.at[k, :, at],
                {"section": halo_sec, "dp": xh * 8 + y * 2 + b},
                halo_send + 2 * i + b, halo_sem + 8 * k + i,
            )
            for b in range(2)
        ]
        halos.extend(copies)

        @pl.when(halo_ok)
        def _():
            for copy in copies:
                copy.start()

    mirror = [{"section": 15 - sec, "dp": xh * 8 + y * 2 + b} for b in range(2)]
    m_out, m_val = alloc(2), [alloc(2), alloc(2)]
    l_out, l_val = alloc(), [alloc(), alloc()]
    mirrors = []
    handed = []

    def share(result, send, land, land_core, n_mirror, n_core):
        copies = [remote(send.at[b], land, mirror[b], n_mirror + b, n_mirror) for b in range(2)]
        mirrors.extend(copies)
        over = remote(result.at[1], land_core, sib, n_core)
        handed.append(over)

        @pl.when(is1)
        def _():
            send[...] = result[...].astype(BF)
            for copy in copies:
                copy.start()

        @pl.when(is0)
        def _():
            over.start()

    stores = []

    def settle(result, land, land_core, n_mirror, n_core, total, target):
        @pl.when(is0)
        def _():
            land_core[...] = result[0]

        @pl.when(is1)
        def _():
            arrive(land_core, n_core)

        arrive(land, n_mirror)
        total[...] = land_core[...] + land[...].astype(F32)
        stores.append(pull(total, target))

    def settle_value(h):
        settle(
            vacc.at[h], mv_r.at[h], lv_r.at[h], m_val[h], l_val[h],
            fin_v.at[h], gval.at[:, pl.ds(h * HALF, HALF)],
        )

    attention(0)
    out_back = push(obk, orx, par)
    ring_sum(1)
    use(0, 0, 0, first=True)
    spread_other(0)
    forward(0, 0)
    attention(1)
    use(0, 1, 0)
    use(0, 0, 1)
    use(0, 0, 3)
    forward(0, 1)
    spread_other(1)
    use(1, 0, 0, first=True)
    use(0, 1, 1)
    use(0, 1, 3)
    far(0, 0)
    use(0, 0, 2)
    use(1, 1, 0)
    forward(1, 0)
    out_back.wait_recv()
    ofin[...] = oacc[: 2 * F].reshape(2, F, H) + orx[...].astype(F32)
    share(ofin, mo_s, mo_r, lo_r, m_out, l_out)
    far(0, 1)
    use(0, 1, 2)
    share(vacc.at[0], mv_s.at[0], mv_r.at[0], lv_r.at[0], m_val[0], l_val[0])
    use(1, 0, 1)
    use(1, 0, 3)
    forward(1, 1)
    use(1, 1, 1)
    use(1, 1, 3)
    settle(ofin, mo_r, lo_r, m_out, l_out, fin_o, gout)
    far(1, 0)
    use(1, 0, 2)
    settle_value(0)
    far(1, 1)
    use(1, 1, 2)
    share(vacc.at[1], mv_s.at[1], mv_r.at[1], lv_r.at[1], m_val[1], l_val[1])

    for copy in sent:
        copy.wait_send()

    @pl.when(halo_ok)
    def _():
        for copy in halos:
            copy.wait_send()

    @pl.when(jnp.logical_not(no_edge))
    def _():
        zero_copy.wait()

    for core, there in ((0, has_above), (1, has_below)):

        @pl.when(there)
        def _(core=core):
            for i in range(8):
                arrive(nxt.at[core, :, pl.ds(i * 256, 256)], halo_sem + 8 * core + i)

    settle_value(1)

    @pl.when(is1)
    def _():
        for copy in mirrors:
            copy.wait_send()

    @pl.when(is0)
    def _():
        for copy in handed:
            copy.wait_send()

    for copy in stores:
        copy.wait()


def on_device(w_value, w_out_t, layer_input, grad_out, heads_out, probs):
    heads = jnp.swapaxes(heads_out[0], 0, 1)
    any_ = pl.BlockSpec(memory_space=pl.ANY)
    scratch = [
        ((4, 4, F, 256), BF),
        ((2, F, 1024), BF),
        ((4, F, H), BF),
        ((4, 2, SEQ, H), BF),
        ((4, 2, 2, SEQ, HALF), BF),
        ((2, 2, SEQ, HALF), F32),
        ((2, 2, SEQ, HALF), BF),
        ((2, 2, 2, SEQ, HALF), BF),
        ((2, 8, SEQ, SEQ), BF),
        ((2, 2, 4, 2, SEQ, HALF), BF),
        ((2, F, T), BF),
        ((2, F, H), BF),
        ((2, 2, F, HALF), F32),
        ((8, 2 * F, 256), F32),
        ((8, 2, F, 256), BF),
        ((4 * F, H), F32),
        ((2, F, H), BF),
        ((2, F, H), BF),
        ((2, F, H), F32),
        ((2, F, H), BF),
        ((F, H), BF),
        ((F, H), F32),
        ((2, 2, F, HALF), BF),
        ((2, F, HALF), BF),
        ((2, F, HALF), F32),
        ((F, H), F32),
        ((2, F, HALF), F32),
        ((F, T), BF),
    ]
    nxt, gval, gout = pl.pallas_call(
        kernel,
        out_shape=(
            jax.ShapeDtypeStruct((2, F, T), BF),
            jax.ShapeDtypeStruct((F, H), F32),
            jax.ShapeDtypeStruct((F, H), F32),
        ),
        in_specs=[any_] * 6,
        out_specs=(any_, any_, any_),
        scratch_shapes=[pltpu.VMEM(shape, dtype) for shape, dtype in scratch]
        + [
            pltpu.SemaphoreType.DMA((N_SEM,)),
            pltpu.SemaphoreType.DMA((N_SEM,)),
            pltpu.SemaphoreType.DMA((N_LOCAL,)),
        ],
        compiler_params=pltpu.CompilerParams(
            collective_id=0, has_side_effects=True, vmem_limit_bytes=52 * 2**20
        ),
        cost_estimate=pl.CostEstimate(
            flops=5_000_000_000, bytes_accessed=8_000_000, transcendentals=0
        ),
    )(w_value[0], w_out_t[0], layer_input[0], grad_out[0], heads, probs[0])
    return nxt[0][None], nxt[1][None], gval[None], gout[None]


def solution(mesh):
    in_specs = (
        P("section", None, "dp", None),
        P("section", None, "dp", None),
        P("section", None, "dp", None),
        P("section", None, "dp", None),
        P("section", "dp", None, None),
        P("section", None, None, "dp", None),
    )
    out_specs = (P("section", "dp", None),) * 4
    return jax.shard_map(
        on_device, mesh=mesh, in_specs=in_specs, out_specs=out_specs, check_vma=False
    )
```

time: 373 us -> 120 us (0.32)
  the two profiles are of different devices: /device:TPU:64 before, /device:TPU:3 now
where the time goes in v1:
time: 120 us
  Pallas kernels  113 us (94%)
  local copies, waits for them, and re-layouts  6.66 us (6%)
    pallas_call x1, Pallas kernels, on_device(): pl.pallas_call(kernel, out_shape=(jax.ShapeDtypeStruct((2, F, T), BF), ja...  113 us
    unnamed x7, local copies, waits for them, and re-layouts  4.28 us

profile of v1, /device:TPU:3, one launch (start us, length us, event | category | flops | bytes accessed | tf_op | source)
XLA Modules:
  0.0 119.9 jit_solution(617987118521392822)
XLA Ops:
  0.6 1.2 copy.12
  1.8 0.0 copy-start
  1.8 1.0 copy-done
  2.8 112.6 %shard_map.93 = (bf16[2,144,2048]{2,1,0:T(8,128)(2,1)}, f32[144,1024]{1,0:T(8,128)S(1)}, f32[144,1024]{1,0:T(8,128)}) custom-call(bf16[2,144,1024]{2,1,0:T(8,128)(2,1)} %bitcast.18, bf16[2,144,1024]{2,1,0:T(8,128)(2,1)} %bitcast.19, bf16[2,144,2048]{2,1,0:T(8,128)(2,1)} %bitcast.16, bf16[2,144,2048]{2,1,0:T(8,128)(2,1)} %bitcast.17, ...), custom_call_target="tpu_custom_call" | custom-call | flops 5000000000 | bytes 8000000 | tf_op jit(solution)/shard_map/pallas_call | solution.py:465
  115.5 2.4 %fusion = (bf16[1,144,2048]{2,1,0:T(8,128)(2,1)}, bf16[1,144,2048]{2,1,0:T(8,128)(2,1)}) fusion(bf16[2,144,2048]{2,1,0:T(8,128)(2,1)} %get-tuple-element.7), kind=kLoop, calls=%fused_computation.1 | loop fusion | bytes 2359296 | tf_op jit(solution)/shard_map/slice | solution.py:487
  117.8 0.0 copy-start.1
  117.8 0.8 copy.15
  118.6 0.5 copy-done.1
  119.1 0.8 copy.16
Async XLA Ops:
  1.8 1.0 copy-start
  117.8 1.3 %copy-start.1 = (f32[144,1024]{1,0:T(8,128)S(1)}, f32[144,1024]{1,0:T(8,128)}, u32[]{:S(2)}) copy-start(f32[144,1024]{1,0:T(8,128)} %get-tuple-element.9) | copy-start | bytes 1769476

commit v2 on v1

--- a/solution.py
+++ b/solution.py
@@ -25,8 +25,8 @@
 
 def kernel(
     w_v, w_o, x_in, g_in, hd_in, pr_in,
-    nxt, gval, gout,
-    gall, goth, wall, hd, sp, own, r1, r2, pb, vall, xb, wvb, vacc, pacc, pbf,
+    ndn, nup, gval, gout,
+    raw, hc, gall, goth, wall, hd, sp, own, r1, r2, pb, vall, xb, wvb, vacc, pacc, pbf,
     oacc, obk, orx, ofin, mo_s, mo_r, lo_r, mv_s, mv_r, lv_r, fin_o, fin_v, zero,
     ssem, rsem, lsem,
 ):
@@ -89,9 +89,9 @@
     def cols(base, yy, width=256):
         return pl.ds(pl.multiple_of(base + yy * 256, 256), width)
 
+    own_hd = pull(hd_in, raw)
     own_w = pull(w_o.at[k], wall.at[k])
     own_g = [pull(g_in.at[k, :, cols(tcol, yy)], gall.at[yy, k]) for yy in range(4)]
-    own_hd = pull(hd_in.at[k], hd.at[y, k])
     own_rest = [
         pull(pr_in.at[k], pb.at[k]),
         pull(w_v.at[k], wvb.at[k]),
@@ -116,25 +116,33 @@
     def _():
         greet({"section": jnp.maximum(sec - 1, 0), "dp": xh * 8 + y * 2 + 1})
 
+    own_hd.wait()
+    for c in range(2):
+        hc[c] = raw[:, c, :]
+    hd[y, k] = hc[k]
     pl.semaphore_wait(barrier, 5 + 2 * k + 2 * halo_ok.astype(jnp.int32))
 
     h_up, h_dn = alloc(2), alloc(2)
-    hd_sib = push(hd_in.at[o], hd.at[y, k], sib)
-    push(hd_in.at[k], hd.at[y, k], up, h_up + k)
-    push(hd_in.at[k], hd.at[y, k], dn, h_dn + k)
+    hd_sib = push(hc.at[o], hd.at[y, k], sib)
+    push(hc.at[k], hd.at[y, k], up, h_up + k)
+    push(hc.at[k], hd.at[y, k], dn, h_dn + k)
     w_copies = [
         push(w_o.at[o], wall.at[k], sib),
         push(w_o.at[k], wall.at[2 + k], par),
         push(w_o.at[o], wall.at[2 + k], pao),
     ]
     g_copies = {}
-    for d in (2, 1, 3, 0):
+
+    def send_g(d):
         yy = around[d]
         g_copies[d] = [
             push(g_in.at[o, :, cols(tcol, yy)], gall.at[yy, k], sib),
             push(g_in.at[k, :, cols(ocol, yy)], gall.at[yy, 2 + k], par),
             push(g_in.at[o, :, cols(ocol, yy)], gall.at[yy, 2 + k], pao),
         ]
+
+    for d in (2, 1, 3, 0):
+        send_g(d)
 
     hd_sib.wait_recv()
     push(hd.at[y, o], hd.at[y, o], up, h_up + o)
@@ -147,13 +155,15 @@
     ]
 
     zero[...] = jnp.zeros_like(zero)
-    edge = jnp.where(has_above, 1, 0)
-    no_edge = jnp.logical_and(has_above, has_below)
-    zero_copy = pltpu.make_async_copy(zero, nxt.at[edge], lsem.at[next(locals_)])
-
-    @pl.when(jnp.logical_not(no_edge))
-    def _():
-        zero_copy.start()
+    zero_sem = next(locals_)
+
+    @pl.when(jnp.logical_not(has_above))
+    def _():
+        pltpu.make_async_copy(zero, ndn, lsem.at[zero_sem]).start()
+
+    @pl.when(jnp.logical_not(has_below))
+    def _():
+        pltpu.make_async_copy(zero, nup, lsem.at[zero_sem]).start()
 
     arrive(hd.at[ym, 0], h_up)
     hd_f_up = push(hd.at[ym, 0], hd.at[ym, 0], up)
@@ -184,10 +194,12 @@
         term = contract(
             gall[around[d]].reshape(4 * F, 256), hd[around[d]].reshape(256, H), 1, 0
         )
-        if first:
-            oacc[...] = term
-        else:
-            oacc[...] += term
+        for h in range(2):
+            half = term[:, h * HALF : (h + 1) * HALF].reshape(4, F, HALF)
+            if first:
+                oacc[h] = half
+            else:
+                oacc[h] += half
 
     s1 = {}
     s2 = {}
@@ -214,25 +226,27 @@
 
     partial(2)
     ring_first(0)
+    ring_first(1)
     partial(1)
     ring_up(0)
-    own_hd.wait()
     arrive(hd.at[yp, 0], h_dn)
     out_term(1, first=True)
     partial(3)
     ring_dn(0)
+    ring_sum(0)
+    ring_up(1)
+    ring_dn(1)
+    ring_sum(1)
     arrive(hd.at[ym, 1], h_up + 1)
     out_term(3)
-    ring_sum(0)
-    ring_first(1)
-    ring_up(1)
-    ring_dn(1)
-    partial(0)
-    out_term(0)
     hd_f_up.wait_recv()
     hd_f_dn.wait_recv()
     out_term(2)
-    obk[...] = oacc[2 * F :].astype(BF).reshape(2, F, H)
+    partial(0)
+    out_term(0)
+    for h in range(2):
+        obk[h] = oacc[h, 2:4].astype(BF)
+    out_back = [push(obk.at[0], orx.at[0], par)]
 
     for copy in own_rest:
         copy.wait()
@@ -253,6 +267,9 @@
                 ).astype(BF)
         mine = vall.at[h, xh, y]
         v_sent[h, "x"] = push(mine, mine, par)
+
+    def spread_own(h):
+        mine = vall.at[h, xh, y]
         v_sent[h, 0, "u"] = push(mine, mine, up)
         v_sent[h, 0, "d"] = push(mine, mine, dn)
 
@@ -298,24 +315,26 @@
         g_here = gall[yy, 0:2] if side == 0 else goth[:, :, cols(0, yy)]
         total = g_here.reshape(2 * F, 256).astype(F32) + (pacc[i] + back)
         pbf[i] = total.astype(BF).reshape(2, F, 256)
-        copies = [
-            remote(
-                pbf.at[i, b], nxt.at[k, :, at],
-                {"section": halo_sec, "dp": xh * 8 + y * 2 + b},
-                halo_send + 2 * i + b, halo_sem + 8 * k + i,
-            )
-            for b in range(2)
-        ]
+        for core, there, out in ((is0, has_below, ndn), (is1, has_above, nup)):
+            copies = [
+                remote(
+                    pbf.at[i, b], out.at[:, at],
+                    {"section": halo_sec, "dp": xh * 8 + y * 2 + b},
+                    halo_send + 2 * i + b, halo_sem + 8 * k + i,
+                )
+                for b in range(2)
+            ]
+
+            @pl.when(jnp.logical_and(core, there))
+            def _(copies=copies):
+                for copy in copies:
+                    copy.start()
+
         halos.extend(copies)
 
-        @pl.when(halo_ok)
-        def _():
-            for copy in copies:
-                copy.start()
-
     mirror = [{"section": 15 - sec, "dp": xh * 8 + y * 2 + b} for b in range(2)]
-    m_out, m_val = alloc(2), [alloc(2), alloc(2)]
-    l_out, l_val = alloc(), [alloc(), alloc()]
+    m_out, m_val = [alloc(2), alloc(2)], [alloc(2), alloc(2)]
+    l_out, l_val = [alloc(), alloc()], [alloc(), alloc()]
     mirrors = []
     handed = []
 
@@ -350,6 +369,20 @@
         total[...] = land_core[...] + land[...].astype(F32)
         stores.append(pull(total, target))
 
+    def share_out(h):
+        out_back[h].wait_recv()
+        ofin[h] = oacc[h, 0:2] + orx[h].astype(F32)
+        share(ofin.at[h], mo_s.at[h], mo_r.at[h], lo_r.at[h], m_out[h], l_out[h])
+
+    def share_value(h):
+        share(vacc.at[h], mv_s.at[h], mv_r.at[h], lv_r.at[h], m_val[h], l_val[h])
+
+    def settle_out(h):
+        settle(
+            ofin.at[h], mo_r.at[h], lo_r.at[h], m_out[h], l_out[h],
+            fin_o.at[h], gout.at[:, pl.ds(h * HALF, HALF)],
+        )
+
     def settle_value(h):
         settle(
             vacc.at[h], mv_r.at[h], lv_r.at[h], m_val[h], l_val[h],
@@ -357,42 +390,43 @@
         )
 
     attention(0)
-    out_back = push(obk, orx, par)
-    ring_sum(1)
+    spread_own(0)
+    out_back.append(push(obk.at[1], orx.at[1], par))
+    attention(1)
+    spread_other(0)
     use(0, 0, 0, first=True)
-    spread_other(0)
+    share_out(0)
+    use(1, 0, 0, first=True)
     forward(0, 0)
-    attention(1)
     use(0, 1, 0)
+    share_out(1)
     use(0, 0, 1)
     use(0, 0, 3)
     forward(0, 1)
+    spread_own(1)
     spread_other(1)
-    use(1, 0, 0, first=True)
+    use(1, 1, 0)
     use(0, 1, 1)
     use(0, 1, 3)
     far(0, 0)
     use(0, 0, 2)
-    use(1, 1, 0)
-    forward(1, 0)
-    out_back.wait_recv()
-    ofin[...] = oacc[: 2 * F].reshape(2, F, H) + orx[...].astype(F32)
-    share(ofin, mo_s, mo_r, lo_r, m_out, l_out)
     far(0, 1)
     use(0, 1, 2)
-    share(vacc.at[0], mv_s.at[0], mv_r.at[0], lv_r.at[0], m_val[0], l_val[0])
+    share_value(0)
+    forward(1, 0)
     use(1, 0, 1)
     use(1, 0, 3)
+    settle_out(0)
     forward(1, 1)
     use(1, 1, 1)
     use(1, 1, 3)
-    settle(ofin, mo_r, lo_r, m_out, l_out, fin_o, gout)
+    settle_out(1)
     far(1, 0)
     use(1, 0, 2)
-    settle_value(0)
     far(1, 1)
     use(1, 1, 2)
-    share(vacc.at[1], mv_s.at[1], mv_r.at[1], lv_r.at[1], m_val[1], l_val[1])
+    share_value(1)
+    settle_value(0)
 
     for copy in sent:
         copy.wait_send()
@@ -402,16 +436,16 @@
         for copy in halos:
             copy.wait_send()
 
-    @pl.when(jnp.logical_not(no_edge))
-    def _():
-        zero_copy.wait()
-
-    for core, there in ((0, has_above), (1, has_below)):
+    @pl.when(jnp.logical_not(jnp.logical_and(has_above, has_below)))
+    def _():
+        pltpu.make_async_copy(zero, ndn, lsem.at[zero_sem]).wait()
+
+    for core, there, out in ((0, has_above, ndn), (1, has_below, nup)):
 
         @pl.when(there)
-        def _(core=core):
+        def _(core=core, out=out):
             for i in range(8):
-                arrive(nxt.at[core, :, pl.ds(i * 256, 256)], halo_sem + 8 * core + i)
+                arrive(out.at[:, pl.ds(i * 256, 256)], halo_sem + 8 * core + i)
 
     settle_value(1)
 
@@ -430,9 +464,10 @@
 
 
 def on_device(w_value, w_out_t, layer_input, grad_out, heads_out, probs):
-    heads = jnp.swapaxes(heads_out[0], 0, 1)
     any_ = pl.BlockSpec(memory_space=pl.ANY)
     scratch = [
+        ((SEQ, 2, H), BF),
+        ((2, SEQ, H), BF),
         ((4, 4, F, 256), BF),
         ((2, F, 1024), BF),
         ((4, F, H), BF),
@@ -448,29 +483,30 @@
         ((2, 2, F, HALF), F32),
         ((8, 2 * F, 256), F32),
         ((8, 2, F, 256), BF),
-        ((4 * F, H), F32),
-        ((2, F, H), BF),
-        ((2, F, H), BF),
-        ((2, F, H), F32),
-        ((2, F, H), BF),
-        ((F, H), BF),
-        ((F, H), F32),
+        ((2, 4, F, HALF), F32),
+        ((2, 2, F, HALF), BF),
+        ((2, 2, F, HALF), BF),
+        ((2, 2, F, HALF), F32),
         ((2, 2, F, HALF), BF),
         ((2, F, HALF), BF),
         ((2, F, HALF), F32),
-        ((F, H), F32),
+        ((2, 2, F, HALF), BF),
+        ((2, F, HALF), BF),
+        ((2, F, HALF), F32),
+        ((2, F, HALF), F32),
         ((2, F, HALF), F32),
         ((F, T), BF),
     ]
-    nxt, gval, gout = pl.pallas_call(
+    down, above, gval, gout = pl.pallas_call(
         kernel,
         out_shape=(
-            jax.ShapeDtypeStruct((2, F, T), BF),
+            jax.ShapeDtypeStruct((F, T), BF),
+            jax.ShapeDtypeStruct((F, T), BF),
             jax.ShapeDtypeStruct((F, H), F32),
             jax.ShapeDtypeStruct((F, H), F32),
         ),
         in_specs=[any_] * 6,
-        out_specs=(any_, any_, any_),
+        out_specs=(any_,) * 4,
         scratch_shapes=[pltpu.VMEM(shape, dtype) for shape, dtype in scratch]
         + [
             pltpu.SemaphoreType.DMA((N_SEM,)),
@@ -478,13 +514,13 @@
             pltpu.SemaphoreType.DMA((N_LOCAL,)),
         ],
         compiler_params=pltpu.CompilerParams(
-            collective_id=0, has_side_effects=True, vmem_limit_bytes=52 * 2**20
+            collective_id=0, has_side_effects=True, vmem_limit_bytes=60 * 2**20
         ),
         cost_estimate=pl.CostEstimate(
             flops=5_000_000_000, bytes_accessed=8_000_000, transcendentals=0
         ),
-    )(w_value[0], w_out_t[0], layer_input[0], grad_out[0], heads, probs[0])
-    return nxt[0][None], nxt[1][None], gval[None], gout[None]
+    )(w_value[0], w_out_t[0], layer_input[0], grad_out[0], heads_out[0], probs[0])
+    return down[None], above[None], gval[None], gout[None]
 
 
 def solution(mesh):

time: 120 us -> 110 us (0.917)
  Pallas kernels: 113 us -> 104 us
  local copies, waits for them, and re-layouts: 6.66 us -> 4.48 us
    pallas_call x1, Pallas kernels: 113 us -> 104 us  [on_device(): pl.pallas_call(kernel, out_shape=(jax.ShapeDtypeStruct((F, T), BF), jax.S...]
    slice x1 -> x0, local copies, waits for them, and re-layouts: 2.38 us -> none  [on_device(): return (nxt[0][None], nxt[1][None], gval[None], gout[None])]
    unnamed x7 -> x10, local copies, waits for them, and re-layouts: 4.28 us -> 4.48 us
where the time goes in v2:
time: 110 us
  Pallas kernels  104 us (95%)
  local copies, waits for them, and re-layouts  4.48 us (4%)
    pallas_call x1, Pallas kernels, on_device(): pl.pallas_call(kernel, out_shape=(jax.ShapeDtypeStruct((F, T), BF), jax.S...  104 us
    unnamed x10, local copies, waits for them, and re-layouts  4.48 us

profile of v2, /device:TPU:3, one launch (start us, length us, event | category | flops | bytes accessed | tf_op | source)
XLA Modules:
  0.0 109.6 jit_solution(12738953967454124080)
XLA Ops:
  0.6 104.4 %shard_map.93 = (bf16[144,2048]{1,0:T(8,128)(2,1)}, bf16[144,2048]{1,0:T(8,128)(2,1)}, f32[144,1024]{1,0:T(8,128)}, f32[144,1024]{1,0:T(8,128)}) custom-call(bf16[2,144,1024]{2,1,0:T(8,128)(2,1)} %bitcast.16, bf16[2,144,1024]{2,1,0:T(8,128)(2,1)} %bitcast.17, bf16[2,144,2048]{2,1,0:T(8,128)(2,1)} %bitcast.14, bf16[2,144,2048]{2,1,0:T(8,128)(2,1)} %bitcast.15, ...), custom_call_target="tpu_custom_call" | custom-call | flops 5000000000 | bytes 8000000 | tf_op jit(solution)/shard_map/pallas_call | solution.py:500
  105.1 0.0 copy-start.2
  105.1 0.0 copy-start.1
  105.1 2.0 %copy.14 = bf16[1,144,2048]{2,1,0:T(8,128)(2,1)} copy(bf16[1,144,2048]{2,1,0:T(8,128)(2,1)} %bitcast.13) | data formatting | bytes 1179648
  107.1 0.0 copy-done.2
  107.1 0.0 copy-start
  107.1 0.8 copy.15
  107.9 0.0 copy-done.1
  107.9 0.8 copy.16
  108.7 0.0 copy-done
  108.7 0.8 copy.17
Async XLA Ops:
  105.1 2.0 %copy-start.2 = (bf16[144,2048]{1,0:T(8,128)(2,1)S(1)}, bf16[144,2048]{1,0:T(8,128)(2,1)}, u32[]{:S(2)}) copy-start(bf16[144,2048]{1,0:T(8,128)(2,1)} %get-tuple-element.9) | copy-start | bytes 1769476
  105.1 2.9 %copy-start.1 = (f32[144,1024]{1,0:T(8,128)S(1)}, f32[144,1024]{1,0:T(8,128)}, u32[]{:S(2)}) copy-start(f32[144,1024]{1,0:T(8,128)} %get-tuple-element.10) | copy-start | bytes 1769476
  107.1 1.6 %copy-start = (f32[144,1024]{1,0:T(8,128)S(1)}, f32[144,1024]{1,0:T(8,128)}, u32[]{:S(2)}) copy-start(f32[144,1024]{1,0:T(8,128)} %get-tuple-element.11) | copy-start | bytes 1769476

commit v3 on v2

--- a/solution.py
+++ b/solution.py
@@ -15,7 +15,7 @@
 HALF = 512
 BF = jnp.bfloat16
 F32 = jnp.float32
-N_SEM = 112
+N_SEM = 136
 N_LOCAL = 20
 
 
@@ -90,7 +90,9 @@
         return pl.ds(pl.multiple_of(base + yy * 256, 256), width)
 
     own_hd = pull(hd_in, raw)
-    own_w = pull(w_o.at[k], wall.at[k])
+    own_w = [
+        pull(w_o.at[k, :, pl.ds(h * HALF, HALF)], wall.at[h, k]) for h in range(2)
+    ]
     own_g = [pull(g_in.at[k, :, cols(tcol, yy)], gall.at[yy, k]) for yy in range(4)]
     own_rest = [
         pull(pr_in.at[k], pb.at[k]),
@@ -126,11 +128,16 @@
     hd_sib = push(hc.at[o], hd.at[y, k], sib)
     push(hc.at[k], hd.at[y, k], up, h_up + k)
     push(hc.at[k], hd.at[y, k], dn, h_dn + k)
-    w_copies = [
-        push(w_o.at[o], wall.at[k], sib),
-        push(w_o.at[k], wall.at[2 + k], par),
-        push(w_o.at[o], wall.at[2 + k], pao),
-    ]
+    w_copies = {}
+
+    def send_w(h):
+        part = pl.ds(h * HALF, HALF)
+        w_copies[h] = [
+            push(w_o.at[o, :, part], wall.at[h, k], sib),
+            push(w_o.at[k, :, part], wall.at[h, 2 + k], par),
+            push(w_o.at[o, :, part], wall.at[h, 2 + k], pao),
+        ]
+
     g_copies = {}
 
     def send_g(d):
@@ -141,8 +148,11 @@
             push(g_in.at[o, :, cols(ocol, yy)], gall.at[yy, 2 + k], pao),
         ]
 
-    for d in (2, 1, 3, 0):
+    send_w(0)
+    for d in (2, 1, 3):
         send_g(d)
+    send_w(1)
+    send_g(0)
 
     hd_sib.wait_recv()
     push(hd.at[y, o], hd.at[y, o], up, h_up + o)
@@ -170,25 +180,26 @@
     arrive(hd.at[yp, 1], h_dn + 1)
     hd_f_dn = push(hd.at[yp, 1], hd.at[yp, 1], dn)
 
-    own_w.wait()
-    for copy in own_g:
+    for copy in own_w + own_g:
         copy.wait()
-    for copy in w_copies:
-        copy.wait_recv()
-
-    def partial(d):
-        for copy in g_copies[d]:
+
+    def weights(h):
+        for copy in w_copies[h]:
             copy.wait_recv()
+
+    def partial(d, h):
+        if h == 0:
+            for copy in g_copies[d]:
+                copy.wait_recv()
         part = contract(
-            gall[around[d]].reshape(4 * F, 256), wall[...].reshape(4 * F, H), 0, 0
+            gall[around[d]].reshape(4 * F, 256), wall[h].reshape(4 * F, HALF), 0, 0
         )
-        for h in range(2):
-            for q in range(2):
-                piece = part[q * SEQ : (q + 1) * SEQ, h * HALF : (h + 1) * HALF]
-                if d == 0:
-                    own[h, q] = piece
-                else:
-                    sp[d, h, q] = piece.astype(BF)
+        for q in range(2):
+            piece = part[q * SEQ : (q + 1) * SEQ]
+            if d == 0:
+                own[h, q] = piece
+            else:
+                sp[d, h, q] = piece.astype(BF)
 
     def out_term(d, first=False):
         term = contract(
@@ -224,29 +235,32 @@
         sp[3, h, 1] = (sp[3, h, 1].astype(F32) + r1[1, h].astype(F32)).astype(BF)
         s2[h, 3] = push(sp.at[3, h, 1], r2.at[1, h, 1], dn)
 
-    partial(2)
-    ring_first(0)
-    ring_first(1)
-    partial(1)
-    ring_up(0)
+    def ring(h):
+        weights(h)
+        partial(2, h)
+        ring_first(h)
+        partial(1, h)
+        ring_up(h)
+        partial(3, h)
+        ring_dn(h)
+
+    ring(0)
+    ring_sum(0)
     arrive(hd.at[yp, 0], h_dn)
     out_term(1, first=True)
-    partial(3)
-    ring_dn(0)
-    ring_sum(0)
-    ring_up(1)
-    ring_dn(1)
-    ring_sum(1)
     arrive(hd.at[ym, 1], h_up + 1)
     out_term(3)
+    ring(1)
     hd_f_up.wait_recv()
     hd_f_dn.wait_recv()
     out_term(2)
-    partial(0)
+    partial(0, 0)
     out_term(0)
     for h in range(2):
         obk[h] = oacc[h, 2:4].astype(BF)
     out_back = [push(obk.at[0], orx.at[0], par)]
+    ring_sum(1)
+    partial(0, 1)
 
     for copy in own_rest:
         copy.wait()
@@ -268,25 +282,31 @@
         mine = vall.at[h, xh, y]
         v_sent[h, "x"] = push(mine, mine, par)
 
-    def spread_own(h):
-        mine = vall.at[h, xh, y]
-        v_sent[h, 0, "u"] = push(mine, mine, up)
-        v_sent[h, 0, "d"] = push(mine, mine, dn)
+    def spread(h, side, late):
+        mine = vall.at[h, (xh, xo)[side], y]
+        for q, way, to in ((late, "u", up), (1 - late, "d", dn)):
+            v_sent[h, side, way, q] = push(mine.at[q], mine.at[q], to)
+
+    def spread_own(h, late):
+        spread(h, 0, late)
 
     def spread_other(h):
         v_sent[h, "x"].wait_recv()
-        other = vall.at[h, xo, y]
-        v_sent[h, 1, "u"] = push(other, other, up)
-        v_sent[h, 1, "d"] = push(other, other, dn)
+        spread(h, 1, 0)
+        spread(h, 1, 1)
 
     def forward(h, side):
         xx = (xh, xo)[side]
-        v_sent[h, side, "u"].wait_recv()
+        v_sent[h, side, "u", 0].wait_recv()
         piece = vall.at[h, xx, ym, 0]
         v_sent[h, side, "fu"] = push(piece, piece, up)
-        v_sent[h, side, "d"].wait_recv()
+        v_sent[h, side, "d", 1].wait_recv()
         piece = vall.at[h, xx, yp, 1]
         v_sent[h, side, "fd"] = push(piece, piece, dn)
+
+    def near(h, side):
+        v_sent[h, side, "u", 1].wait_recv()
+        v_sent[h, side, "d", 0].wait_recv()
 
     def far(h, side):
         v_sent[h, side, "fu"].wait_recv()
@@ -390,39 +410,45 @@
         )
 
     attention(0)
-    spread_own(0)
+    spread_own(0, 0)
+    spread_own(0, 1)
     out_back.append(push(obk.at[1], orx.at[1], par))
     attention(1)
     spread_other(0)
+    forward(0, 0)
+    share_out(0)
     use(0, 0, 0, first=True)
-    share_out(0)
     use(1, 0, 0, first=True)
-    forward(0, 0)
+    spread_own(1, 0)
     use(0, 1, 0)
-    share_out(1)
+    near(0, 0)
     use(0, 0, 1)
     use(0, 0, 3)
     forward(0, 1)
-    spread_own(1)
+    spread_own(1, 1)
     spread_other(1)
+    share_out(1)
     use(1, 1, 0)
+    far(0, 0)
+    use(0, 0, 2)
+    near(0, 1)
     use(0, 1, 1)
     use(0, 1, 3)
-    far(0, 0)
-    use(0, 0, 2)
     far(0, 1)
     use(0, 1, 2)
     share_value(0)
     forward(1, 0)
+    near(1, 0)
     use(1, 0, 1)
     use(1, 0, 3)
     settle_out(0)
     forward(1, 1)
+    far(1, 0)
+    use(1, 0, 2)
+    settle_out(1)
+    near(1, 1)
     use(1, 1, 1)
     use(1, 1, 3)
-    settle_out(1)
-    far(1, 0)
-    use(1, 0, 2)
     far(1, 1)
     use(1, 1, 2)
     share_value(1)
@@ -460,6 +486,19 @@
             copy.wait_send()
 
     for copy in stores:
+        copy.wait()
+
+
+def hand_over(*refs):
+    inputs, outputs, held, sems = refs[:4], refs[4:8], refs[8:12], refs[12]
+    reads = [pltpu.make_async_copy(inputs[i], held[i], sems.at[i]) for i in range(4)]
+    writes = [pltpu.make_async_copy(held[i], outputs[i], sems.at[4 + i]) for i in range(4)]
+    for copy in reads:
+        copy.start()
+    for read, write in zip(reads, writes):
+        read.wait()
+        write.start()
+    for copy in writes:
         copy.wait()
 
 
@@ -470,7 +509,7 @@
         ((2, SEQ, H), BF),
         ((4, 4, F, 256), BF),
         ((2, F, 1024), BF),
-        ((4, F, H), BF),
+        ((2, 4, F, HALF), BF),
         ((4, 2, SEQ, H), BF),
         ((4, 2, 2, SEQ, HALF), BF),
         ((2, 2, SEQ, HALF), F32),
@@ -520,7 +559,18 @@
             flops=5_000_000_000, bytes_accessed=8_000_000, transcendentals=0
         ),
     )(w_value[0], w_out_t[0], layer_input[0], grad_out[0], heads_out[0], probs[0])
-    return down[None], above[None], gval[None], gout[None]
+    shapes = tuple(
+        jax.ShapeDtypeStruct(a.shape, a.dtype) for a in (down, above, gval, gout)
+    )
+    results = pl.pallas_call(
+        hand_over,
+        out_shape=shapes,
+        in_specs=[any_] * 4,
+        out_specs=(any_,) * 4,
+        scratch_shapes=[pltpu.VMEM(a.shape, a.dtype) for a in shapes]
+        + [pltpu.SemaphoreType.DMA((8,))],
+    )(down, above, gval, gout)
+    return tuple(a[None] for a in results)
 
 
 def solution(mesh):

time: 110 us -> 108 us (0.982)
  local copies, waits for them, and re-layouts: 4.48 us -> 0 us
  Pallas kernels: 104 us -> 107 us
    unnamed x10 -> x0, local copies, waits for them, and re-layouts: 4.48 us -> none
    pallas_call x0 -> x1, Pallas kernels: none -> 2.53 us  [on_device(): pl.pallas_call(hand_over, out_shape=shapes, in_specs=[any_] * 4, out_spec...]
where the time goes in v3:
time: 108 us
  Pallas kernels  107 us (99%)
    pallas_call x1, Pallas kernels, on_device(): pl.pallas_call(kernel, out_shape=(jax.ShapeDtypeStruct((F, T), BF), jax.S...  105 us
    pallas_call x1, Pallas kernels, on_device(): pl.pallas_call(hand_over, out_shape=shapes, in_specs=[any_] * 4, out_spec...  2.53 us

profile of v3, /device:TPU:3, one launch (start us, length us, event | category | flops | bytes accessed | tf_op | source)
XLA Modules:
  0.0 108.1 jit_solution(18012543932835835490)
XLA Ops:
  0.6 104.9 %shard_map.93 = (bf16[144,2048]{1,0:T(8,128)(2,1)}, bf16[144,2048]{1,0:T(8,128)(2,1)}, f32[144,1024]{1,0:T(8,128)}, f32[144,1024]{1,0:T(8,128)}) custom-call(bf16[2,144,1024]{2,1,0:T(8,128)(2,1)} %bitcast.12, bf16[2,144,1024]{2,1,0:T(8,128)(2,1)} %bitcast.13, bf16[2,144,2048]{2,1,0:T(8,128)(2,1)} %bitcast.10, bf16[2,144,2048]{2,1,0:T(8,128)(2,1)} %bitcast.11, ...), custom_call_target="tpu_custom_call" | custom-call | flops 5000000000 | bytes 8000000 | tf_op jit(solution)/shard_map/pallas_call | solution.py:539
  105.6 2.5 %shard_map.94 = (bf16[144,2048]{1,0:T(8,128)(2,1)}, bf16[144,2048]{1,0:T(8,128)(2,1)}, f32[144,1024]{1,0:T(8,128)}, f32[144,1024]{1,0:T(8,128)}) custom-call(bf16[144,2048]{1,0:T(8,128)(2,1)} %get-tuple-element.12.refs_0_, bf16[144,2048]{1,0:T(8,128)(2,1)} %get-tuple-element.13.refs_1_, f32[144,1024]{1,0:T(8,128)} %get-tuple-element.14.refs_2_, ...), custom_call_target="tpu_custom_call" | custom-call | tf_op jit(solution)/shard_map/pallas_call | solution.py:565

commit v4 on v3

--- a/solution.py
+++ b/solution.py
@@ -108,7 +108,7 @@
 
     for to in (sib, par, pao, up, dn):
         greet(to)
-    greet({"section": 15 - sec, "dp": xh * 8 + y * 2 + 1})
+    greet({"section": 15 - sec, "dp": dp})
 
     @pl.when(has_above)
     def _():
@@ -122,7 +122,7 @@
     for c in range(2):
         hc[c] = raw[:, c, :]
     hd[y, k] = hc[k]
-    pl.semaphore_wait(barrier, 5 + 2 * k + 2 * halo_ok.astype(jnp.int32))
+    pl.semaphore_wait(barrier, 6 + 2 * halo_ok.astype(jnp.int32))
 
     h_up, h_dn = alloc(2), alloc(2)
     hd_sib = push(hc.at[o], hd.at[y, k], sib)
@@ -352,27 +352,35 @@
 
         halos.extend(copies)
 
-    mirror = [{"section": 15 - sec, "dp": xh * 8 + y * 2 + b} for b in range(2)]
+    mirror = {"section": 15 - sec, "dp": dp}
     m_out, m_val = [alloc(2), alloc(2)], [alloc(2), alloc(2)]
     l_out, l_val = [alloc(), alloc()], [alloc(), alloc()]
     mirrors = []
     handed = []
+    handed_1 = []
 
     def share(result, send, land, land_core, n_mirror, n_core):
-        copies = [remote(send.at[b], land, mirror[b], n_mirror + b, n_mirror) for b in range(2)]
-        mirrors.extend(copies)
+        mirrors.append(remote(send.at[1], land, mirror, n_mirror))
+        between = remote(send.at[0], send.at[1], sib, n_mirror + 1)
+        handed_1.append(between)
         over = remote(result.at[1], land_core, sib, n_core)
         handed.append(over)
 
         @pl.when(is1)
-        def _():
+        def _(across=mirrors[-1]):
             send[...] = result[...].astype(BF)
-            for copy in copies:
-                copy.start()
+            between.start()
+            across.start()
 
         @pl.when(is0)
         def _():
             over.start()
+
+    def pass_on(send, land, n_mirror):
+        @pl.when(is0)
+        def _():
+            arrive(send.at[1], n_mirror + 1)
+            remote(send.at[1], land, mirror, n_mirror).start()
 
     stores = []
 
@@ -396,6 +404,12 @@
 
     def share_value(h):
         share(vacc.at[h], mv_s.at[h], mv_r.at[h], lv_r.at[h], m_val[h], l_val[h])
+
+    def pass_out(h):
+        pass_on(mo_s.at[h], mo_r.at[h], m_out[h])
+
+    def pass_value(h):
+        pass_on(mv_s.at[h], mv_r.at[h], m_val[h])
 
     def settle_out(h):
         settle(
@@ -419,6 +433,7 @@
     share_out(0)
     use(0, 0, 0, first=True)
     use(1, 0, 0, first=True)
+    pass_out(0)
     spread_own(1, 0)
     use(0, 1, 0)
     near(0, 0)
@@ -429,6 +444,7 @@
     spread_other(1)
     share_out(1)
     use(1, 1, 0)
+    pass_out(1)
     far(0, 0)
     use(0, 0, 2)
     near(0, 1)
@@ -439,6 +455,7 @@
     share_value(0)
     forward(1, 0)
     near(1, 0)
+    pass_value(0)
     use(1, 0, 1)
     use(1, 0, 3)
     settle_out(0)
@@ -452,6 +469,7 @@
     far(1, 1)
     use(1, 1, 2)
     share_value(1)
+    pass_value(1)
     settle_value(0)
 
     for copy in sent:
@@ -475,9 +493,12 @@
 
     settle_value(1)
 
+    for copy in mirrors:
+        copy.wait_send()
+
     @pl.when(is1)
     def _():
-        for copy in mirrors:
+        for copy in handed_1:
             copy.wait_send()
 
     @pl.when(is0)

time: 108 us -> 105 us (0.972)
  Pallas kernels: 107 us -> 105 us
    pallas_call x1, Pallas kernels: 105 us -> 102 us  [on_device(): pl.pallas_call(kernel, out_shape=(jax.ShapeDtypeStruct((F, T), BF), jax.S...]
where the time goes in v4:
time: 105 us
  Pallas kernels  105 us (100%)
    pallas_call x1, Pallas kernels, on_device(): pl.pallas_call(kernel, out_shape=(jax.ShapeDtypeStruct((F, T), BF), jax.S...  102 us
    pallas_call x1, Pallas kernels, on_device(): pl.pallas_call(hand_over, out_shape=shapes, in_specs=[any_] * 4, out_spec...  2.53 us

profile of v4, /device:TPU:3, one launch (start us, length us, event | category | flops | bytes accessed | tf_op | source)
XLA Modules:
  0.0 105.3 jit_solution(7770006623313088010)
XLA Ops:
  0.6 102.1 %shard_map.93 = (bf16[144,2048]{1,0:T(8,128)(2,1)}, bf16[144,2048]{1,0:T(8,128)(2,1)}, f32[144,1024]{1,0:T(8,128)}, f32[144,1024]{1,0:T(8,128)}) custom-call(bf16[2,144,1024]{2,1,0:T(8,128)(2,1)} %bitcast.12, bf16[2,144,1024]{2,1,0:T(8,128)(2,1)} %bitcast.13, bf16[2,144,2048]{2,1,0:T(8,128)(2,1)} %bitcast.10, bf16[2,144,2048]{2,1,0:T(8,128)(2,1)} %bitcast.11, ...), custom_call_target="tpu_custom_call" | custom-call | flops 5000000000 | bytes 8000000 | tf_op jit(solution)/shard_map/pallas_call | solution.py:560
  102.7 2.5 %shard_map.94 = (bf16[144,2048]{1,0:T(8,128)(2,1)}, bf16[144,2048]{1,0:T(8,128)(2,1)}, f32[144,1024]{1,0:T(8,128)}, f32[144,1024]{1,0:T(8,128)}) custom-call(bf16[144,2048]{1,0:T(8,128)(2,1)} %get-tuple-element.12.refs_0_, bf16[144,2048]{1,0:T(8,128)(2,1)} %get-tuple-element.13.refs_1_, f32[144,1024]{1,0:T(8,128)} %get-tuple-element.14.refs_2_, ...), custom_call_target="tpu_custom_call" | custom-call | tf_op jit(solution)/shard_map/pallas_call | solution.py:586
